TPU v7x, 128 devices: a whole 4x4x4 slice. The times are simulated.
128 devices in a mesh: seq: 16 (over y, x_lo, core), chan: 8 (over z, x_hi).
Axes of the slice: x: 4 (x_hi: 2, x_lo: 2; x = x_hi * 2 + x_lo), y: 4, z: 4, core: 2. Of those that a mesh axis runs over, the one named last changes fastest.
Arguments:
- signal: bfloat16 [512, 65536], P('chan', 'seq'), may hold values from -6 to 6
- gate: bfloat16 [512, 65536], P('chan', 'seq'), may hold values from -6 to 6
- spec_real: float32 [512, 32, 4096], P('chan', 'seq'), may hold values from -6 to 6
- spec_imag: float32 [512, 32, 4096], P('chan', 'seq'), may hold values from -6 to 6
- skip_gain: float32 [512], P('chan'), may hold values from 0.5 to 1.5
- mix_weight: bfloat16 [512, 512], P('chan'), may hold values from -0.25 to 0.25
Outputs:
- mixed: bfloat16 [512, 65536], P('chan', 'seq')
All inputs are finite; a program needn't handle non-finite values.
Results may differ from a plain program's by a relative error of at most 0.0049.
Values may be sent and summed in bfloat16 or wider, within the bound.
A program may use at most 128 MiB of HBM per device.

v0:
```python
import functools

import jax
import jax.numpy as jnp
import numpy as np
from jax import lax
from jax.experimental import pallas as pl
from jax.experimental.pallas import tpu as pltpu
from jax.sharding import PartitionSpec as P

BF = jnp.bfloat16
F32 = jnp.float32
N = 131072


def unit(numer, period):
    angle = 2.0 * np.pi * (np.asarray(numer, np.int64) % period) / period
    return np.cos(angle), np.sin(angle)


def tables():
    r = np.arange(32)
    a = np.arange(16)
    i, h, jb = np.meshgrid(np.arange(4), np.arange(2), np.arange(16), indexing="ij")
    s1 = (4 * (16 * h + jb) + i).reshape(-1)
    m2 = np.arange(128)
    m1 = np.arange(32)
    s2 = np.arange(32)
    eye16 = np.eye(16)
    eye4 = np.eye(4)
    c, s = unit(r[:, None] * a[None, :], 32)
    k0 = np.concatenate([np.kron(c, eye16), np.kron(-s, eye16)], 0)
    k0i = np.concatenate([np.kron(c.T, eye16), np.kron(-s.T, eye16)], 1)
    klow = 32 * m2[None, :] + r[:, None]
    c, s = unit(klow[:, :, None] * s1[None, None, :], 4096)
    m = np.concatenate([np.concatenate([c, s], 2), np.concatenate([-s, c], 2)], 1)
    mi = np.swapaxes(m, 1, 2)
    c, s = unit(klow[:, :, None] * np.tile(s2, 4)[None, None, :], N)
    tw = np.stack([c, s], 1)
    twi = np.swapaxes(tw, 2, 3)
    c, s = unit(m1[:, None] * s2[None, :], 32)
    c, s = np.kron(eye4, c), np.kron(eye4, s)
    l2 = np.concatenate([np.concatenate([c, s], 1), np.concatenate([-s, c], 1)], 0)
    l2i = l2.T
    perm = np.zeros((4, 4, 32, 4, 4, 32))
    for ci in range(4):
        for ii in range(4):
            perm[ci, ii, np.arange(32), ii, ci, np.arange(32)] = 1
    perm = perm.reshape(512, 512)
    return dict(k0=k0, k0i=k0i / N, m=m, mi=mi, tw=tw, twi=twi, l2=l2, l2i=l2i, perm=perm)


def split(x):
    x = np.asarray(x, np.float32)
    hi = x.astype(jnp.bfloat16)
    lo = (x - hi.astype(np.float32)).astype(jnp.bfloat16)
    return hi, lo


def dot(a, b):
    return lax.dot_general(a, b, (((1,), (0,)), ((), ())), preferred_element_type=F32)


def dot_nt(a, b):
    return lax.dot_general(a, b, (((1,), (1,)), ((), ())), preferred_element_type=F32)


def conv_kernel(x_ref, hre_ref, him_ref, k0_ref, k0i_ref, m_ref, mi_ref, tw_ref, twi_ref,
                l2_ref, l2i_ref, perm_ref, permi_ref, out_ref, dsc, osc):
    xa = jnp.concatenate([x_ref[:, c].reshape(512, 128) for c in range(4)], axis=1)
    spread = dot(xa, perm_ref[...]).astype(BF).reshape(16, 32, 512)
    for h in range(2):
        rows = spread[:, h * 16:(h + 1) * 16].reshape(256, 512)
        d = (dot(k0_ref[0], rows) + dot(k0_ref[1], rows)).astype(BF)
        for ri in range(2):
            for i in range(4):
                dsc[:, pl.ds(ri * 128 + i * 32 + h * 16, 16), :] = d[
                    ri * 512:(ri + 1) * 512, i * 128:(i + 1) * 128].reshape(32, 16, 128)

    def one(r):
        e = dot(m_ref[r], dsc[r])
        er, ei = e[:128], e[128:]
        c, s = tw_ref[r, 0], tw_ref[r, 1]
        ec = jnp.concatenate([er * c + ei * s, ei * c - er * s], axis=1).astype(BF)
        f = dot_nt(l2_ref[...], ec)
        fr, fi = f[:128], f[128:]
        hr, hi = hre_ref[r].astype(F32), him_ref[r].astype(F32)
        p = jnp.concatenate([fr * hr - fi * hi, fr * hi + fi * hr], axis=0).astype(BF)
        g = dot(l2i_ref[...], p)
        gr, gi = g[:128], g[128:]
        c, s = twi_ref[r, 0], twi_ref[r, 1]
        gc = jnp.concatenate([gr * c - gi * s, gi * c + gr * s], axis=1).astype(BF)
        o = dot_nt(mi_ref[r], gc).astype(BF)
        for ri in range(2):
            for i in range(4):
                for h in range(2):
                    osc[h, pl.ds(pl.multiple_of(ri * 512 + r * 16, 16), 16), pl.ds(i * 128, 128)] = (
                        o[ri * 128 + i * 32 + h * 16:ri * 128 + i * 32 + h * 16 + 16])

    def step(t, carry):
        for u in range(4):
            one(t * 4 + u)
        return carry

    lax.fori_loop(0, 8, step, 0)
    halves = []
    for h in range(2):
        back = dot(k0i_ref[0], osc[h]) + dot(k0i_ref[1], osc[h])
        halves.append((back * (1.0 / N)).astype(BF))
    for h in range(2):
        y = dot(halves[h], permi_ref[...]).astype(BF).reshape(16, 16, 512)
        for c in range(4):
            out_ref[:, c, pl.ds(h * 16, 16), :] = y[:, :, c * 128:(c + 1) * 128]


def constants():
    t = tables()
    pair = lambda v: np.stack(split(v))
    one = lambda v: np.asarray(v, np.float32).astype(jnp.bfloat16)
    f = lambda v: np.asarray(v, np.float32)
    return [pair(t["k0"]), pair(t["k0i"] * N), one(t["m"]), one(t["mi"]), f(t["tw"]), f(t["twi"]),
            one(t["l2"]), one(t["l2i"]), one(t["perm"]), one(t["perm"].T)]


def conv_local(x, hre, him, interpret=False):
    consts = [jnp.asarray(v) for v in constants()]
    return pl.pallas_call(
        conv_kernel,
        out_shape=jax.ShapeDtypeStruct((16, 4, 32, 128), BF),
        in_specs=[pl.BlockSpec(memory_space=pltpu.VMEM)] * 13,
        out_specs=pl.BlockSpec(memory_space=pltpu.VMEM),
        scratch_shapes=[pltpu.VMEM((32, 256, 128), BF), pltpu.VMEM((2, 1024, 512), BF)],
        compiler_params=pltpu.CompilerParams(vmem_limit_bytes=56 * 1024 * 1024),
        cost_estimate=pl.CostEstimate(flops=10**10, bytes_accessed=2 * 10**7, transcendentals=0),
        interpret=interpret,
    )(x, hre, him, *consts)


def body(signal, gate, spec_real, spec_imag, skip_gain, mix_weight):
    swap = functools.partial(lax.all_to_all, axis_name="seq", split_axis=0, concat_axis=0)
    x = swap(signal.reshape(4, 16, 32, 128).transpose(1, 0, 2, 3))
    deal = lambda v: swap(
        v.reshape(4, 16, 2, 32, 128).transpose(1, 2, 0, 3, 4).astype(BF).reshape(16, 256, 128)
    ).reshape(32, 128, 128)
    conv = swap(conv_local(x, deal(spec_real), deal(spec_imag)))
    conv = conv.transpose(1, 0, 2, 3).reshape(64, 4096).astype(F32)
    direct = conv + skip_gain[:, None] * signal.astype(F32)
    gated = (gate.astype(F32) * direct).astype(BF)
    result = jnp.dot(
        mix_weight,
        lax.all_gather(gated, "chan", axis=0, tiled=True),
        preferred_element_type=F32,
    )
    return result.astype(BF)


def solution(mesh):
    placed = (
        P("chan", "seq"),
        P("chan", "seq"),
        P("chan", "seq", None),
        P("chan", "seq", None),
        P("chan"),
        P("chan", None),
    )
    return jax.shard_map(
        body, mesh=mesh, in_specs=placed, out_specs=P("chan", "seq"), check_vma=False
    )
```

profile of v0, /device:TPU:0, one launch (start us, length us, event | category | flops | bytes accessed | tf_op | source)
XLA Modules:
  0.0 192.5 jit_solution(2380513357881007948)
XLA Ops:
  6.5 0.0 copy-start
  6.5 0.0 copy-start.1
  6.5 1.3 copy.23
  7.8 0.8 copy_bitcast_fusion
  8.7 5.6 %all-to-all-start = ((bf16[16,4,32,128]{3,2,1,0:T(8,128)(2,1)}), bf16[16,4,32,128]{3,2,1,0:T(8,128)(2,1)}, u32[]{:S(2)}, u32[]{:S(2)}) async-start(bf16[16,4,32,128]{3,2,1,0:T(8,128)(2,1)} %copy_bitcast_fusion), calls=%async_computation | async-start | bytes 1048576 | tf_op jit(solution)/shard_map/all_to_all | solution.py:141
  14.3 0.0 copy-done.1
  14.3 0.9 convert_element_type.43
  15.2 0.8 convert_element_type.44
  16.0 0.0 copy-start.2
  16.1 1.1 copy.20
  17.2 8.0 %all-to-all-done.x_ref = bf16[16,4,32,128]{3,2,1,0:T(8,128)(2,1)} async-done(((bf16[16,4,32,128]{3,2,1,0:T(8,128)(2,1)}), bf16[16,4,32,128]{3,2,1,0:T(8,128)(2,1)}, u32[]{:S(2)}, u32[]{:S(2)}) %all-to-all-start) | async-done | bytes 524320 | tf_op jit(solution)/shard_map/all_to_all | solution.py:141
  25.2 4.3 %all-to-all-start.1 = ((bf16[16,256,128]{2,1,0:T(8,128)(2,1)}), bf16[16,256,128]{2,1,0:T(8,128)(2,1)}, u32[]{:S(2)}, u32[]{:S(2)}) async-start(bf16[16,256,128]{2,1,0:T(8,128)(2,1)} %bitcast.2), calls=%async_computation.1 | async-start | bytes 2097152 | tf_op jit(solution)/shard_map/all_to_all | solution.py:142
  29.6 0.0 all-gather.2.cloned.1.call-start
  29.7 0.0 copy-done.2
  29.7 0.9 convert_element_type.46
  30.5 0.8 convert_element_type.47
  31.4 0.1 copy.21
  31.5 14.7 %all-to-all-done.1 = bf16[16,256,128]{2,1,0:T(8,128)(2,1)} async-done(((bf16[16,256,128]{2,1,0:T(8,128)(2,1)}), bf16[16,256,128]{2,1,0:T(8,128)(2,1)}, u32[]{:S(2)}, u32[]{:S(2)}) %all-to-all-start.1) | async-done | bytes 1048608 | tf_op jit(solution)/shard_map/all_to_all | solution.py:142
  46.2 19.8 %all_to_all.20 = bf16[16,256,128]{2,1,0:T(8,128)(2,1)} all-to-all(bf16[16,256,128]{2,1,0:T(8,128)(2,1)S(1)} %bitcast.29), channel_id=1, replica_groups=mesh['seq'=16,'chan'=8] {'seq'}, dimensions={0} | all-to-all | bytes 2097152 | tf_op jit(solution)/shard_map/all_to_all | solution.py:142
  66.0 28.1 %shard_map.154 = bf16[16,4,32,128]{3,2,1,0:T(8,128)(2,1)} custom-call(bf16[16,4,32,128]{3,2,1,0:T(8,128)(2,1)} %all-to-all-done.x_ref, bf16[32,128,128]{2,1,0:T(8,128)(2,1)} %bitcast.3.hre_ref, bf16[32,128,128]{2,1,0:T(8,128)(2,1)} %bitcast.35, bf16[2,1024,256]{2,1,0:T(8,128)(2,1)} %constant.18.clone.k0_ref, bf16[2,256,1024]{2,1,0:T(8,128)(2,1)} %constant.19.clone.k0i_ref, ...), custom_call_target="tpu_custom_call" | custom-call | flops 10000000000 | bytes 20000000 | tf_op jit(solution)/shard_map/pallas_call | solution.py:127
  94.1 0.0 copy-start.3
  94.1 0.0 copy-start.4
  94.1 0.0 copy-start.5
  94.1 14.5 %all_to_all.21 = bf16[16,4,32,128]{3,2,1,0:T(8,128)(2,1)S(1)} all-to-all(bf16[16,4,32,128]{3,2,1,0:T(8,128)(2,1)} %shard_map.154), channel_id=1, replica_groups=mesh['seq'=16,'chan'=8] {'seq'}, dimensions={0} | all-to-all | bytes 1048576 | tf_op jit(solution)/shard_map/all_to_all | solution.py:145
  108.6 0.1 convert_bitcast_fusion
  108.8 0.1 copy.22
  108.9 0.0 copy-done.3
  108.9 0.0 copy-done.4
  108.9 0.0 copy-done.5
  108.9 1.5 fusion.2
  110.4 0.0 all-gather.2.cloned.1.call-update
  110.4 71.4 %all-gather.2.cloned.1.call-done = bf16[512,4096]{1,0:T(8,128)(2,1)} async-done(((bf16[64,4096]{1,0:T(8,128)(2,1)}), bf16[512,4096]{1,0:T(8,128)(2,1)}) %all-gather.2.cloned.1.call-update) | async-done | bytes 4194320 | tf_op jit(solution)/shard_map/all_gather | solution.py:151
  181.8 0.0 copy-done
  181.8 3.8 %fusion = bf16[64,4096]{1,0:T(8,128)(2,1)} fusion(bf16[64,512]{1,0:T(8,128)(2,1)S(1)} %copy-done, bf16[512,4096]{1,0:T(8,128)(2,1)} %all-gather.2.cloned.1.call-done), kind=kOutput, calls=%fused_computation.1 | convolution fusion | flops 268697600 | bytes 4784128 | tf_op jit(solution)/shard_map/dot_general | solution.py:149
Async XLA Ops:
  6.5 175.3 %copy-start = (bf16[64,512]{1,0:T(8,128)(2,1)S(1)}, bf16[64,512]{1,0:T(8,128)(2,1)}, u32[]{:S(2)}) copy-start(bf16[64,512]{1,0:T(8,128)(2,1)} %param.21) | copy-start | bytes 196612
  6.5 7.8 %copy-start.1 = (f32[64,2,4096]{2,1,0:T(2,128)S(1)}, f32[64,2,4096]{2,1,0:T(2,128)}, u32[]{:S(2)}) copy-start(f32[64,2,4096]{2,1,0:T(2,128)} %param.18) | copy-start | bytes 6291460
  8.7 16.6 %all-to-all-start = ((bf16[16,4,32,128]{3,2,1,0:T(8,128)(2,1)}), bf16[16,4,32,128]{3,2,1,0:T(8,128)(2,1)}, u32[]{:S(2)}, u32[]{:S(2)}) async-start(bf16[16,4,32,128]{3,2,1,0:T(8,128)(2,1)} %copy_bitcast_fusion), calls=%async_computation | async-start | bytes 1048576 | tf_op jit(solution)/shard_map/all_to_all | solution.py:141
  16.0 13.6 %copy-start.2 = (f32[64,2,4096]{2,1,0:T(2,128)S(1)}, f32[64,2,4096]{2,1,0:T(2,128)}, u32[]{:S(2)}) copy-start(f32[64,2,4096]{2,1,0:T(2,128)} %param.19) | copy-start | bytes 6291460
  25.2 21.0 %all-to-all-start.1 = ((bf16[16,256,128]{2,1,0:T(8,128)(2,1)}), bf16[16,256,128]{2,1,0:T(8,128)(2,1)}, u32[]{:S(2)}, u32[]{:S(2)}) async-start(bf16[16,256,128]{2,1,0:T(8,128)(2,1)} %bitcast.2), calls=%async_computation.1 | async-start | bytes 2097152 | tf_op jit(solution)/shard_map/all_to_all | solution.py:142
  29.6 152.2 %all-gather.2.cloned.1.call-start = ((), (), s32[]{:S(2)}) async-start(), calls=%async_computation.4 | async-start | bytes 4718592 | tf_op jit(solution)/shard_map/all_gather | solution.py:151
  94.1 14.8 %copy-start.3 = (bf16[64,4096]{1,0:T(8,128)(2,1)S(1)}, bf16[64,4096]{1,0:T(8,128)(2,1)}, u32[]{:S(2)}) copy-start(bf16[64,4096]{1,0:T(8,128)(2,1)} %param.16) | copy-start | bytes 1572868
  94.1 14.8 %copy-start.4 = (bf16[64,4096]{1,0:T(8,128)(2,1)S(1)}, bf16[64,4096]{1,0:T(8,128)(2,1)}, u32[]{:S(2)}) copy-start(bf16[64,4096]{1,0:T(8,128)(2,1)} %param.17) | copy-start | bytes 1572868
  94.1 14.8 %copy-start.5 = (f32[64]{0:T(128)S(1)}, f32[64]{0:T(128)}, u32[]{:S(2)}) copy-start(f32[64]{0:T(128)} %param.20) | copy-start | bytes 772
Sparse Core Ops, SparseCore 0:
  110.5 71.2 all-gather.1
where the time goes:
time: 193 us
  waiting for transfers between devices  94.2 us (49%)
  blocking collectives  34.3 us (18%)
  Pallas kernels  28.1 us (15%)
  between operations  13.5 us (7%)
  starting transfers between devices  10 us (5%)
  local copies, waits for them, and re-layouts  5.16 us (3%)
  matrix products  3.83 us (2%)
  other arithmetic  3.33 us (2%)
    all_gather x1, waiting for transfers between devices, body(): lax.all_gather(gated, 'chan', axis=0, tiled=True)  71.4 us
    pallas_call x1, Pallas kernels, conv_local(): pl.pallas_call(conv_kernel, out_shape=jax.ShapeDtypeStruct((16, 4, 32, 12...  28.1 us
    all_to_all x1, blocking collectives, body(): swap(v.reshape(4, 16, 2, 32, 128).transpose(1, 2, 0, 3, 4).astype(BF).res...  19.8 us
    all_to_all x1, waiting for transfers between devices, body(): swap(v.reshape(4, 16, 2, 32, 128).transpose(1, 2, 0, 3, 4).astype(BF).res...  14.7 us
    all_to_all x1, blocking collectives, body(): conv = swap(conv_local(x, deal(spec_real), deal(spec_imag)))  14.5 us
    all_to_all x1, waiting for transfers between devices, body(): x = swap(signal.reshape(4, 16, 32, 128).transpose(1, 0, 2, 3))  8.05 us
    all_to_all x1, starting transfers between devices, body(): x = swap(signal.reshape(4, 16, 32, 128).transpose(1, 0, 2, 3))  5.64 us
    all_to_all x1, starting transfers between devices, body(): swap(v.reshape(4, 16, 2, 32, 128).transpose(1, 2, 0, 3, 4).astype(BF).res...  4.35 us
  transfers between devices with their start and end apart: 3, of which 3 were waited for; matrix products, arithmetic and copies ran while one was open for 2% of the time, Pallas kernels for 0%

commit v1 on v0

v1 whole, which is shorter than its diff:
```python
import jax
import jax.numpy as jnp
import numpy as np
from jax import lax
from jax.experimental import pallas as pl
from jax.experimental.pallas import tpu as pltpu
from jax.sharding import PartitionSpec as P

BF = jnp.bfloat16
F32 = jnp.float32
N = 131072
SEQ_N = 16
CHAN_N = 8
MESH = pl.DeviceIdType.MESH


def unit(numer, period):
    angle = 2.0 * np.pi * (np.asarray(numer, np.int64) % period) / period
    return np.cos(angle), np.sin(angle)


def tables():
    r = np.arange(32)
    a = np.arange(16)
    i, h, jb = np.meshgrid(np.arange(4), np.arange(2), np.arange(16), indexing="ij")
    s1 = (4 * (16 * h + jb) + i).reshape(-1)
    m2 = np.arange(128)
    m1 = np.arange(32)
    s2 = np.arange(32)
    eye16 = np.eye(16)
    eye4 = np.eye(4)
    c, s = unit(r[:, None] * a[None, :], 32)
    k0 = np.concatenate([np.kron(c, eye16), np.kron(-s, eye16)], 0)
    k0i = np.concatenate([np.kron(c.T, eye16), np.kron(-s.T, eye16)], 1)
    klow = 32 * m2[None, :] + r[:, None]
    c, s = unit(klow[:, :, None] * s1[None, None, :], 4096)
    m = np.concatenate([np.concatenate([c, s], 2), np.concatenate([-s, c], 2)], 1)
    mi = np.swapaxes(m, 1, 2)
    c, s = unit(klow[:, :, None] * np.tile(s2, 4)[None, None, :], N)
    tw = np.stack([c, s], 1)
    twi = np.swapaxes(tw, 2, 3)[:, :, :64]
    c, s = unit(m1[:, None] * s2[None, :], 32)
    c, s = np.kron(eye4, c), np.kron(eye4, s)
    l2 = np.concatenate([np.concatenate([c, s], 1), np.concatenate([-s, c], 1)], 0)
    c, s = unit(s2[:, None] * m1[None, :], 32)
    c, s = np.kron(np.eye(2), c), np.kron(np.eye(2), s)
    l2i = np.concatenate([np.concatenate([c, -s], 1), np.concatenate([s, c], 1)], 0)
    perm = np.zeros((4, 4, 32, 4, 4, 32))
    for ci in range(4):
        for ii in range(4):
            perm[ci, ii, np.arange(32), ii, ci, np.arange(32)] = 1
    perm = perm.reshape(512, 512)
    permi = np.zeros((4, 2, 32, 2, 4, 32))
    for ci in range(2):
        for ii in range(4):
            permi[ii, ci, np.arange(32), ci, ii, np.arange(32)] = 1
    permi = permi.reshape(256, 256)
    return k0, k0i, m, mi, tw, twi, l2, l2i, perm, permi


def split(x):
    x = np.asarray(x, np.float32)
    hi = x.astype(jnp.bfloat16)
    lo = (x - hi.astype(np.float32)).astype(jnp.bfloat16)
    return hi, lo


def constants():
    k0, k0i, m, mi, tw, twi, l2, l2i, perm, permi = tables()
    pair = lambda v: np.stack(split(v))
    one = lambda v: np.asarray(v, np.float32).astype(jnp.bfloat16)
    f = lambda v: np.asarray(v, np.float32)
    return [pair(k0), pair(k0i), one(m), one(mi), f(tw), f(twi), one(l2), one(l2i), one(perm), one(permi)]


def dot(a, b):
    return lax.dot_general(a, b, (((1,), (0,)), ((), ())), preferred_element_type=F32)


def dot_nt(a, b):
    return lax.dot_general(a, b, (((1,), (1,)), ((), ())), preferred_element_type=F32)


def kernel(sig_hbm, gate_hbm, hre_hbm, him_hbm, gain_ref, w_ref,
           k0_hbm, k0i_hbm, m_hbm, mi_hbm, tw_hbm, twi_hbm, l2_hbm, l2i_hbm, perm_hbm, permi_hbm,
           out_ref,
           sig, gate, h32, k0, k0i, m, mi, tw, twi, l2, l2i, perm, permi,
           s32, sx, xr, hs, hr, dsc, fsc, osc, cs, cr, c32, gt, acc,
           load_sem, xs_sem, xr_sem, hs_sem, hr_sem, cs_sem, cr_sem, gs_sem, gr_sem):
    me = lax.axis_index("seq")
    mc = lax.axis_index("chan")
    peer = [lax.rem(me + d, SEQ_N) for d in range(SEQ_N)]
    source = [lax.rem(me - d + SEQ_N, SEQ_N) for d in range(SEQ_N)]
    other = [lax.rem(mc + d, CHAN_N) for d in range(CHAN_N)]
    origin = [lax.rem(mc - d + CHAN_N, CHAN_N) for d in range(CHAN_N)]

    barrier = pltpu.get_barrier_semaphore()
    for d in range(1, SEQ_N):
        pl.semaphore_signal(barrier, inc=1, device_id=(peer[d], mc), device_id_type=MESH)
    for d in range(1, CHAN_N):
        pl.semaphore_signal(barrier, inc=1, device_id=(me, other[d]), device_id_type=MESH)

    pairs = [(sig_hbm, sig), (hre_hbm, h32.at[0]), (him_hbm, h32.at[1]), (perm_hbm, perm), (k0_hbm, k0),
             (m_hbm, m), (l2_hbm, l2), (tw_hbm, tw), (l2i_hbm, l2i), (twi_hbm, twi), (mi_hbm, mi),
             (k0i_hbm, k0i), (permi_hbm, permi), (gate_hbm, gate)]
    loads = [pltpu.make_async_copy(a, b, load_sem.at[n]) for n, (a, b) in enumerate(pairs)]
    for copy in loads:
        copy.start()

    loads[0].wait()
    for c in range(4):
        for j in range(32):
            s32[c, pl.ds(j, 16, stride=32), :] = sig[c * 16:(c + 1) * 16, j * 128:(j + 1) * 128].astype(F32)
    for c in range(4):
        sx[:, c] = s32[c].astype(BF).reshape(16, 32, 128)
    pl.semaphore_wait(barrier, SEQ_N + CHAN_N - 2)
    x_out = []
    for d in range(1, SEQ_N):
        copy = pltpu.make_async_remote_copy(
            src_ref=sx.at[peer[d]], dst_ref=xr.at[me], send_sem=xs_sem.at[d], recv_sem=xr_sem.at[d],
            device_id=(peer[d], mc), device_id_type=MESH)
        copy.start()
        x_out.append(copy)
    xr[me] = sx[me]

    loads[1].wait()
    loads[2].wait()
    h_out = []
    for g in range(2):
        for d in list(range(1, SEQ_N)) + [0]:
            for part in range(2):
                for i in range(2):
                    for cl in range(2):
                        row = pl.multiple_of(((2 * g + cl) * 16 + peer[d]) * 64, 64) + i
                        val = h32[part, pl.ds(row, 32, stride=2), :].astype(BF)
                        if d == 0:
                            hr[g, me, part, i, pl.ds(cl * 32, 32), :] = val
                        else:
                            hs[g, d, part, i, pl.ds(cl * 32, 32), :] = val
            if d:
                copy = pltpu.make_async_remote_copy(
                    src_ref=hs.at[g, d], dst_ref=hr.at[g, me], send_sem=hs_sem.at[g, d],
                    recv_sem=hr_sem.at[g, d], device_id=(peer[d], mc), device_id_type=MESH)
                copy.start()
                h_out.append(copy)

    for n in range(3, 8):
        loads[n].wait()
    for copy in x_out:
        copy.wait_recv()
    xa = jnp.concatenate([xr[:, c].reshape(512, 128) for c in range(4)], axis=1)
    spread = dot(xa, perm[...]).astype(BF).reshape(16, 32, 512)
    for h in range(2):
        rows = spread[:, h * 16:(h + 1) * 16].reshape(256, 512)
        dv = (dot(k0[0], rows) + dot(k0[1], rows)).astype(BF)
        for ri in range(2):
            for i in range(4):
                dsc[:, pl.ds(ri * 128 + i * 32 + h * 16, 16), :] = dv[
                    ri * 512:(ri + 1) * 512, i * 128:(i + 1) * 128].reshape(32, 16, 128)

    def forward(t, carry):
        ecs = []
        for u in range(4):
            r = t * 4 + u
            e = dot(m[r], dsc[r])
            er, ei = e[:128], e[128:]
            c, s = tw[r, 0], tw[r, 1]
            ecs.append(jnp.concatenate([er * c + ei * s, ei * c - er * s], axis=1).astype(BF))
        for u in range(0, 4, 2):
            f = dot_nt(l2[...], jnp.concatenate(ecs[u:u + 2], axis=0))
            fsc[t * 4 + u] = f[:, :128]
            fsc[t * 4 + u + 1] = f[:, 128:]
        return carry

    lax.fori_loop(0, 8, forward, 0)
    for n in range(8, 14):
        loads[n].wait()
    low = lax.broadcasted_iota(jnp.int32, (32, 128), 1) < 64

    def inverse_of(g, q):
        ps = []
        for i in range(2):
            r = 2 * q + i
            fr = fsc[r, pl.ds(g * 64, 64), :]
            fi = fsc[r, pl.ds(128 + g * 64, 64), :]
            re, im = hr[g, q, 0, i].astype(F32), hr[g, q, 1, i].astype(F32)
            ps.append(jnp.concatenate([fr * re - fi * im, fr * im + fi * re], axis=0).astype(BF))
        gv = dot(l2i[...], jnp.concatenate(ps, axis=1))
        for i in range(2):
            r = 2 * q + i
            gr, gi = gv[:64, i * 128:(i + 1) * 128], gv[64:, i * 128:(i + 1) * 128]
            c, s = twi[r, 0], twi[r, 1]
            gc = jnp.concatenate([gr * c - gi * s, gi * c + gr * s], axis=1).astype(BF)
            o = dot_nt(mi[r], jnp.concatenate([gc, gc], axis=0))
            for ri in range(2):
                for k in range(2):
                    at = ri * 128 + k * 64
                    val = jnp.where(low, o[at:at + 32], o[at + 32:at + 64]).astype(BF)
                    for h in range(2):
                        osc[g, h, pl.ds(pl.multiple_of(ri * 512 + r * 16, 16), 16), pl.ds(k * 128, 128)] = (
                            val[h * 16:(h + 1) * 16])

    def inverse_step(g):
        def step(d, carry):
            q = lax.rem(me - d + SEQ_N, SEQ_N)
            pltpu.make_async_remote_copy(
                src_ref=hs.at[g, d], dst_ref=hr.at[g, q], send_sem=hs_sem.at[g, d],
                recv_sem=hr_sem.at[g, d], device_id=(me, mc), device_id_type=MESH).wait_recv()
            inverse_of(g, q)
            return carry
        return step

    def inverse_end(g):
        for h in range(2):
            back = dot(k0i[0], osc[g, h]) + dot(k0i[1], osc[g, h])
            y = dot((back * (1.0 / N)).astype(BF), permi[...]).astype(BF).reshape(16, 16, 256)
            for cl in range(2):
                cs[g, :, cl, pl.ds(h * 16, 16), :] = y[:, :, cl * 128:(cl + 1) * 128]
        sent = []
        for d in range(1, SEQ_N):
            copy = pltpu.make_async_remote_copy(
                src_ref=cs.at[g, peer[d]], dst_ref=cr.at[g, me], send_sem=cs_sem.at[g, d],
                recv_sem=cr_sem.at[g, d], device_id=(peer[d], mc), device_id_type=MESH)
            copy.start()
            sent.append(copy)
        cr[g, me] = cs[g, me]
        return sent

    def gating(g, arrivals):
        for copy in arrivals:
            copy.wait_recv()
        for cl in range(2):
            c32[cl] = cr[g, :, cl].reshape(512, 128).astype(F32)
        for cl in range(2):
            at = (2 * g + cl) * 16
            gain = gain_ref[at:at + 16, :]
            for j in range(32):
                lanes = slice(j * 128, (j + 1) * 128)
                direct = c32[cl, pl.ds(j, 16, stride=32), :] + gain * sig[at:at + 16, lanes].astype(F32)
                gt[g, mc, pl.ds(cl * 16, 16), lanes] = (gate[at:at + 16, lanes].astype(F32) * direct).astype(BF)
        sent = []
        for d in range(1, CHAN_N):
            copy = pltpu.make_async_remote_copy(
                src_ref=gt.at[g, mc], dst_ref=gt.at[g, mc], send_sem=gs_sem.at[g, d],
                recv_sem=gr_sem.at[g, d], device_id=(me, other[d]), device_id_type=MESH)
            copy.start()
            sent.append(copy)
        return sent

    inverse_of(0, me)
    lax.fori_loop(1, SEQ_N, inverse_step(0), 0)
    conv_a = inverse_end(0)
    inverse_of(1, me)
    lax.fori_loop(1, 9, inverse_step(1), 0)
    gather_a = gating(0, conv_a)
    lax.fori_loop(9, SEQ_N, inverse_step(1), 0)
    conv_b = inverse_end(1)
    gather_b = gating(1, conv_b)

    def mixing(g, arrivals):
        for copy in arrivals:
            copy.wait_recv()
        for j in range(8):
            lanes = slice(j * 512, (j + 1) * 512)
            part = dot(w_ref[g], gt[g, :, :, lanes].reshape(32 * CHAN_N, 512))
            if g == 0:
                acc[:, lanes] = part
            else:
                out_ref[:, lanes] = (acc[:, lanes] + part).astype(BF)

    mixing(0, gather_a)
    mixing(1, gather_b)
    for copy in x_out + h_out + conv_a + conv_b + gather_a + gather_b:
        copy.wait_send()


def body(signal, gate, spec_real, spec_imag, skip_gain, mix_weight):
    consts = [jnp.asarray(v) for v in constants()]
    rows = lambda v: v.reshape(64, 2, 32, 128).transpose(0, 2, 1, 3).reshape(4096, 128)
    gain = jnp.broadcast_to(skip_gain[:, None], (64, 128))
    weight = mix_weight.reshape(64, CHAN_N, 2, 32).transpose(2, 0, 1, 3).reshape(2, 64, 32 * CHAN_N)
    anywhere = pl.BlockSpec(memory_space=pl.ANY)
    vmem = pl.BlockSpec(memory_space=pltpu.VMEM)
    buf = lambda *shape: pltpu.VMEM(shape, BF)
    wide = lambda *shape: pltpu.VMEM(shape, F32)
    dma = lambda *shape: pltpu.SemaphoreType.DMA(shape)
    held = [pltpu.VMEM(v.shape, v.dtype) for v in consts]
    return pl.pallas_call(
        kernel,
        out_shape=jax.ShapeDtypeStruct((64, 4096), BF),
        in_specs=[anywhere] * 4 + [vmem] * 2 + [anywhere] * len(consts),
        out_specs=vmem,
        scratch_shapes=[buf(64, 4096), buf(64, 4096), wide(2, 4096, 128)] + held + [
            wide(4, 512, 128), buf(16, 4, 32, 128), buf(16, 4, 32, 128),
            buf(2, 16, 2, 2, 64, 128), buf(2, 16, 2, 2, 64, 128), buf(32, 256, 128), wide(32, 256, 128),
            buf(2, 2, 1024, 256), buf(2, 16, 2, 32, 128), buf(2, 16, 2, 32, 128), wide(2, 512, 128),
            buf(2, CHAN_N, 32, 4096), wide(64, 4096),
            dma(14), dma(16), dma(16), dma(2, 16), dma(2, 16), dma(2, 16), dma(2, 16), dma(2, 8), dma(2, 8)],
        compiler_params=pltpu.CompilerParams(
            collective_id=0, has_side_effects=True, vmem_limit_bytes=60 * 1024 * 1024),
        cost_estimate=pl.CostEstimate(flops=10**10, bytes_accessed=3 * 10**7, transcendentals=0),
    )(signal, gate, rows(spec_real), rows(spec_imag), gain, weight, *consts)


def solution(mesh):
    placed = (
        P("chan", "seq"),
        P("chan", "seq"),
        P("chan", "seq", None),
        P("chan", "seq", None),
        P("chan"),
        P("chan", None),
    )
    return jax.shard_map(
        body, mesh=mesh, in_specs=placed, out_specs=P("chan", "seq"), check_vma=False
    )
```

time: 193 us -> 105 us (0.54)
  waiting for transfers between devices: 94.2 us -> 0 us
  Pallas kernels: 28.1 us -> 99.7 us
  blocking collectives: 34.3 us -> 0 us
  between operations: 13.5 us -> 0.02 us
  starting transfers between devices: 10 us -> 0 us
  matrix products: 3.83 us -> 0 us
  other arithmetic: 3.33 us -> 0 us
    pallas_call x1, Pallas kernels: 28.1 us -> 99.7 us  [body(): pl.pallas_call(kernel, out_shape=jax.ShapeDtypeStruct((64, 4096), BF), in...]
    all_gather x1 -> x0, waiting for transfers between devices: 71.4 us -> none  [body(): lax.all_gather(gated, 'chan', axis=0, tiled=True)]
    all_to_all x2 -> x0, blocking collectives: 34.3 us -> none  [the longest x1 19.8 us: body(): swap(v.reshape(4, 16, 2, 32, 128).transpose(1, 2, 0, 3, 4).astype(BF).res...]
    all_to_all x2 -> x0, waiting for transfers between devices: 22.8 us -> none  [the longest x1 14.7 us: body(): swap(v.reshape(4, 16, 2, 32, 128).transpose(1, 2, 0, 3, 4).astype(BF).res...]
    all_to_all x2 -> x0, starting transfers between devices: 9.99 us -> none  [the longest x1 5.64 us: body(): x = swap(signal.reshape(4, 16, 32, 128).transpose(1, 0, 2, 3))]
    dot_general x1 -> x0, matrix products: 3.83 us -> none  [body(): jnp.dot(mix_weight, lax.all_gather(gated, 'chan', axis=0, tiled=True), pr...]
    convert_element_type x4 -> x0, other arithmetic: 3.33 us -> none  [the longest x2 1.73 us: body(): v.reshape(4, 16, 2, 32, 128).transpose(1, 2, 0, 3, 4).astype(BF)]
    convert_element_type x5 -> x0, local copies, waits for them, and re-layouts: 3.01 us -> none  [the longest x4 2.92 us: body(): v.reshape(4, 16, 2, 32, 128).transpose(1, 2, 0, 3, 4).astype(BF)]
  transfers between devices with their start and end apart: 3 -> 0, of which waited for: 3 -> 0; matrix products, arithmetic and copies ran while one was open for 2% -> 0% of each run, Pallas kernels for 0% -> 0%
where the time goes in v1:
time: 105 us
  Pallas kernels  99.7 us (95%)
  local copies, waits for them, and re-layouts  4.89 us (5%)
    pallas_call x1, Pallas kernels, body(): pl.pallas_call(kernel, out_shape=jax.ShapeDtypeStruct((64, 4096), BF), in...  99.7 us
    unnamed x2, local copies, waits for them, and re-layouts  2.82 us

profile of v1, /device:TPU:0, one launch (start us, length us, event | category | flops | bytes accessed | tf_op | source)
XLA Modules:
  0.0 104.6 jit_solution(4207308344590461979)
XLA Ops:
  0.0 1.3 %broadcast_in_dim.2.gain_ref = f32[64,128]{1,0:T(8,128)} broadcast(f32[64]{0:T(128)} %param.20), dimensions={0} | broadcast | bytes 33024 | tf_op jit(solution)/shard_map/broadcast_in_dim | solution.py:280
  1.3 1.0 copy.22
  2.3 0.7 copy.24.w_ref
  3.0 99.7 %shard_map.154 = bf16[64,4096]{1,0:T(8,128)(2,1)} custom-call(bf16[64,4096]{1,0:T(8,128)(2,1)} %sig_hbm.1, bf16[64,4096]{1,0:T(8,128)(2,1)} %gate_hbm.1, f32[4096,128]{1,0:T(8,128)} %bitcast.16, f32[4096,128]{1,0:T(8,128)} %bitcast.17, f32[64,128]{1,0:T(8,128)} %broadcast_in_dim.2.gain_ref, bf16[2,64,256]{2,1,0:T(8,128)(2,1)} %copy.24.w_ref, ...), custom_call_target="tpu_custom_call" | custom-call | flops 10000000000 | bytes 30000000 | tf_op jit(solution)/shard_map/pallas_call | solution.py:288
  102.8 1.9 %copy.26 = bf16[64,4096]{1,0:T(8,128)(2,1)} copy(bf16[64,4096]{1,0:T(8,128)(2,1)} %shard_map.154) | data formatting | bytes 1048576
  (1 shorter events, 0.0 us)

commit v2 on v1

--- a/solution.py
+++ b/solution.py
@@ -85,20 +85,21 @@
            k0_hbm, k0i_hbm, m_hbm, mi_hbm, tw_hbm, twi_hbm, l2_hbm, l2i_hbm, perm_hbm, permi_hbm,
            out_ref,
            sig, gate, h32, k0, k0i, m, mi, tw, twi, l2, l2i, perm, permi,
-           s32, sx, xr, hs, hr, dsc, fsc, osc, cs, cr, c32, gt, acc,
+           s32, sx, xr, hs, hr, dsc, fsc, osc, cs, cr, c32, gt,
            load_sem, xs_sem, xr_sem, hs_sem, hr_sem, cs_sem, cr_sem, gs_sem, gr_sem):
     me = lax.axis_index("seq")
     mc = lax.axis_index("chan")
     peer = [lax.rem(me + d, SEQ_N) for d in range(SEQ_N)]
     source = [lax.rem(me - d + SEQ_N, SEQ_N) for d in range(SEQ_N)]
-    other = [lax.rem(mc + d, CHAN_N) for d in range(CHAN_N)]
-    origin = [lax.rem(mc - d + CHAN_N, CHAN_N) for d in range(CHAN_N)]
+    flip = lambda c: c + 1 - 2 * lax.rem(c, 2)
+    pc = flip(mc)
+    upc, dnc = lax.rem(mc + 2, CHAN_N), lax.rem(mc + 6, CHAN_N)
 
     barrier = pltpu.get_barrier_semaphore()
     for d in range(1, SEQ_N):
         pl.semaphore_signal(barrier, inc=1, device_id=(peer[d], mc), device_id_type=MESH)
-    for d in range(1, CHAN_N):
-        pl.semaphore_signal(barrier, inc=1, device_id=(me, other[d]), device_id_type=MESH)
+    for c in (pc, upc, dnc):
+        pl.semaphore_signal(barrier, inc=1, device_id=(me, c), device_id_type=MESH)
 
     pairs = [(sig_hbm, sig), (hre_hbm, h32.at[0]), (him_hbm, h32.at[1]), (perm_hbm, perm), (k0_hbm, k0),
              (m_hbm, m), (l2_hbm, l2), (tw_hbm, tw), (l2i_hbm, l2i), (twi_hbm, twi), (mi_hbm, mi),
@@ -107,13 +108,16 @@
     for copy in loads:
         copy.start()
 
+    square = lax.broadcasted_iota(jnp.int32, (64, 64), 0) == lax.broadcasted_iota(jnp.int32, (64, 64), 1)
+    gain_col = jnp.sum(jnp.where(square, gain_ref[...], 0.0), axis=1, keepdims=True)
+
     loads[0].wait()
     for c in range(4):
         for j in range(32):
             s32[c, pl.ds(j, 16, stride=32), :] = sig[c * 16:(c + 1) * 16, j * 128:(j + 1) * 128].astype(F32)
     for c in range(4):
         sx[:, c] = s32[c].astype(BF).reshape(16, 32, 128)
-    pl.semaphore_wait(barrier, SEQ_N + CHAN_N - 2)
+    pl.semaphore_wait(barrier, SEQ_N + 2)
     x_out = []
     for d in range(1, SEQ_N):
         copy = pltpu.make_async_remote_copy(
@@ -233,52 +237,65 @@
             c32[cl] = cr[g, :, cl].reshape(512, 128).astype(F32)
         for cl in range(2):
             at = (2 * g + cl) * 16
-            gain = gain_ref[at:at + 16, :]
+            gain = gain_col[at:at + 16]
             for j in range(32):
                 lanes = slice(j * 128, (j + 1) * 128)
                 direct = c32[cl, pl.ds(j, 16, stride=32), :] + gain * sig[at:at + 16, lanes].astype(F32)
-                gt[g, mc, pl.ds(cl * 16, 16), lanes] = (gate[at:at + 16, lanes].astype(F32) * direct).astype(BF)
-        sent = []
-        for d in range(1, CHAN_N):
-            copy = pltpu.make_async_remote_copy(
-                src_ref=gt.at[g, mc], dst_ref=gt.at[g, mc], send_sem=gs_sem.at[g, d],
-                recv_sem=gr_sem.at[g, d], device_id=(me, other[d]), device_id_type=MESH)
-            copy.start()
-            sent.append(copy)
-        return sent
+                gt[mc, g, pl.ds(cl * 16, 16), lanes] = (gate[at:at + 16, lanes].astype(F32) * direct).astype(BF)
+
+    gathered = []
+    every, first, second = pl.ds(0, 32), pl.ds(0, 16), pl.ds(16, 16)
+
+    def pass_on(g, block, rows, to, n):
+        copy = pltpu.make_async_remote_copy(
+            src_ref=gt.at[block, g, rows], dst_ref=gt.at[block, g, rows], send_sem=gs_sem.at[g, n],
+            recv_sem=gr_sem.at[g, n], device_id=(me, to), device_id_type=MESH)
+        copy.start()
+        gathered.append(copy)
+        return copy
+
+    def spread_own(g):
+        return [pass_on(g, mc, every, pc, 0), pass_on(g, mc, every, upc, 1), pass_on(g, mc, every, dnc, 2)]
+
+    def spread_partner(g, own):
+        own[0].wait_recv()
+        partner = [pass_on(g, pc, every, upc, 3), pass_on(g, pc, every, dnc, 4)]
+        own[1].wait_recv()
+        own[2].wait_recv()
+        return partner + [pass_on(g, dnc, first, upc, 5), pass_on(g, upc, second, dnc, 6)]
+
+    def spread_last(g, partner):
+        partner[0].wait_recv()
+        partner[1].wait_recv()
+        return partner[2:] + [pass_on(g, flip(dnc), first, upc, 7), pass_on(g, flip(upc), second, dnc, 8)]
 
     inverse_of(0, me)
     lax.fori_loop(1, SEQ_N, inverse_step(0), 0)
     conv_a = inverse_end(0)
     inverse_of(1, me)
     lax.fori_loop(1, 9, inverse_step(1), 0)
-    gather_a = gating(0, conv_a)
+    gating(0, conv_a)
+    own_a = spread_own(0)
     lax.fori_loop(9, SEQ_N, inverse_step(1), 0)
     conv_b = inverse_end(1)
-    gather_b = gating(1, conv_b)
-
-    def mixing(g, arrivals):
-        for copy in arrivals:
-            copy.wait_recv()
-        for j in range(8):
-            lanes = slice(j * 512, (j + 1) * 512)
-            part = dot(w_ref[g], gt[g, :, :, lanes].reshape(32 * CHAN_N, 512))
-            if g == 0:
-                acc[:, lanes] = part
-            else:
-                out_ref[:, lanes] = (acc[:, lanes] + part).astype(BF)
-
-    mixing(0, gather_a)
-    mixing(1, gather_b)
-    for copy in x_out + h_out + conv_a + conv_b + gather_a + gather_b:
+    partner_a = spread_partner(0, own_a)
+    gating(1, conv_b)
+    own_b = spread_own(1)
+    last_a = spread_last(0, partner_a)
+    partner_b = spread_partner(1, own_b)
+    last_b = spread_last(1, partner_b)
+    for copy in last_a + last_b:
+        copy.wait_recv()
+    for j in range(8):
+        lanes = slice(j * 512, (j + 1) * 512)
+        out_ref[:, lanes] = dot(w_ref[...], gt[:, :, :, lanes].reshape(512, 512)).astype(BF)
+    for copy in x_out + h_out + conv_a + conv_b + gathered:
         copy.wait_send()
 
 
 def body(signal, gate, spec_real, spec_imag, skip_gain, mix_weight):
     consts = [jnp.asarray(v) for v in constants()]
     rows = lambda v: v.reshape(64, 2, 32, 128).transpose(0, 2, 1, 3).reshape(4096, 128)
-    gain = jnp.broadcast_to(skip_gain[:, None], (64, 128))
-    weight = mix_weight.reshape(64, CHAN_N, 2, 32).transpose(2, 0, 1, 3).reshape(2, 64, 32 * CHAN_N)
     anywhere = pl.BlockSpec(memory_space=pl.ANY)
     vmem = pl.BlockSpec(memory_space=pltpu.VMEM)
     buf = lambda *shape: pltpu.VMEM(shape, BF)
@@ -294,12 +311,12 @@
             wide(4, 512, 128), buf(16, 4, 32, 128), buf(16, 4, 32, 128),
             buf(2, 16, 2, 2, 64, 128), buf(2, 16, 2, 2, 64, 128), buf(32, 256, 128), wide(32, 256, 128),
             buf(2, 2, 1024, 256), buf(2, 16, 2, 32, 128), buf(2, 16, 2, 32, 128), wide(2, 512, 128),
-            buf(2, CHAN_N, 32, 4096), wide(64, 4096),
-            dma(14), dma(16), dma(16), dma(2, 16), dma(2, 16), dma(2, 16), dma(2, 16), dma(2, 8), dma(2, 8)],
+            buf(CHAN_N, 2, 32, 4096),
+            dma(14), dma(16), dma(16), dma(2, 16), dma(2, 16), dma(2, 16), dma(2, 16), dma(2, 9), dma(2, 9)],
         compiler_params=pltpu.CompilerParams(
             collective_id=0, has_side_effects=True, vmem_limit_bytes=60 * 1024 * 1024),
         cost_estimate=pl.CostEstimate(flops=10**10, bytes_accessed=3 * 10**7, transcendentals=0),
-    )(signal, gate, rows(spec_real), rows(spec_imag), gain, weight, *consts)
+    )(signal, gate, rows(spec_real), rows(spec_imag), skip_gain.reshape(1, 64), mix_weight, *consts)
 
 
 def solution(mesh):

time: 105 us -> 86.5 us (0.82)
  Pallas kernels: 99.7 us -> 84.4 us
  local copies, waits for them, and re-layouts: 4.89 us -> 1.87 us
    pallas_call x1, Pallas kernels: 99.7 us -> 84.4 us  [body(): pl.pallas_call(kernel, out_shape=jax.ShapeDtypeStruct((64, 4096), BF), in...]
    broadcast_in_dim x1 -> x0, local copies, waits for them, and re-layouts: 1.33 us -> none  [body(): gain = jnp.broadcast_to(skip_gain[:, None], (64, 128))]
    unnamed x2 -> x1, local copies, waits for them, and re-layouts: 2.82 us -> 1.87 us
where the time goes in v2:
time: 86.5 us; the launch traced here: 86.3 us
  Pallas kernels  84.4 us (98%)
  local copies, waits for them, and re-layouts  1.87 us (2%)
    pallas_call x1, Pallas kernels, body(): pl.pallas_call(kernel, out_shape=jax.ShapeDtypeStruct((64, 4096), BF), in...  84.4 us
    unnamed x1, local copies, waits for them, and re-layouts  1.87 us

profile of v2, /device:TPU:0, one launch (start us, length us, event | category | flops | bytes accessed | tf_op | source)
XLA Modules:
  0.0 86.3 jit_solution(11802458262805516515)
XLA Ops:
  0.0 84.4 %shard_map.154 = bf16[64,4096]{1,0:T(8,128)(2,1)} custom-call(bf16[64,4096]{1,0:T(8,128)(2,1)} %sig_hbm.1, bf16[64,4096]{1,0:T(8,128)(2,1)} %gate_hbm.1, f32[4096,128]{1,0:T(8,128)} %bitcast.11, f32[4096,128]{1,0:T(8,128)} %bitcast.12, f32[1,64]{1,0:T(1,128)} %bitcast.13, bf16[64,512]{1,0:T(8,128)(2,1)} %w_ref.1, ...), custom_call_target="tpu_custom_call" | custom-call | flops 10000000000 | bytes 30000000 | tf_op jit(solution)/shard_map/pallas_call | solution.py:305
  84.4 1.9 %copy.20 = bf16[64,4096]{1,0:T(8,128)(2,1)} copy(bf16[64,4096]{1,0:T(8,128)(2,1)} %shard_map.154) | data formatting | bytes 1048576

commit v3 on v2

--- a/solution.py
+++ b/solution.py
@@ -11,6 +11,8 @@
 N = 131072
 SEQ_N = 16
 CHAN_N = 8
+CHUNKS = (1, 4)
+SPLIT = 9
 MESH = pl.DeviceIdType.MESH
 
 
@@ -85,14 +87,14 @@
            k0_hbm, k0i_hbm, m_hbm, mi_hbm, tw_hbm, twi_hbm, l2_hbm, l2i_hbm, perm_hbm, permi_hbm,
            out_ref,
            sig, gate, h32, k0, k0i, m, mi, tw, twi, l2, l2i, perm, permi,
-           s32, sx, xr, hs, hr, dsc, fsc, osc, cs, cr, c32, gt,
-           load_sem, xs_sem, xr_sem, hs_sem, hr_sem, cs_sem, cr_sem, gs_sem, gr_sem):
+           s32, sx, xr, hs, hr, dsc, fsc, osc, cs, cr, c32, gt, wp, acc, ps, pr,
+           load_sem, xs_sem, xr_sem, hs_sem, hr_sem, cs_sem, cr_sem, gs_sem, gr_sem, ps_sem, pr_sem):
     me = lax.axis_index("seq")
     mc = lax.axis_index("chan")
     peer = [lax.rem(me + d, SEQ_N) for d in range(SEQ_N)]
     source = [lax.rem(me - d + SEQ_N, SEQ_N) for d in range(SEQ_N)]
-    flip = lambda c: c + 1 - 2 * lax.rem(c, 2)
-    pc = flip(mc)
+    xh, mz = lax.rem(mc, 2), lax.div(mc, 2)
+    pc = mc + 1 - 2 * xh
     upc, dnc = lax.rem(mc + 2, CHAN_N), lax.rem(mc + 6, CHAN_N)
 
     barrier = pltpu.get_barrier_semaphore()
@@ -126,10 +128,27 @@
         copy.start()
         x_out.append(copy)
     xr[me] = sx[me]
+    w_copy = pltpu.make_async_remote_copy(
+        src_ref=w_ref, dst_ref=wp, send_sem=ps_sem.at[4], recv_sem=pr_sem.at[4],
+        device_id=(me, pc), device_id_type=MESH)
+    w_copy.start()
 
     loads[1].wait()
     loads[2].wait()
-    h_out = []
+
+    def filter_copy(g, d):
+        return pltpu.make_async_remote_copy(
+            src_ref=hs.at[g, d], dst_ref=hr.at[g, me], send_sem=hs_sem.at[g, d],
+            recv_sem=hr_sem.at[g, d], device_id=(peer[d], mc), device_id_type=MESH)
+
+    def start_filter(g):
+        for d in range(1, SEQ_N):
+            filter_copy(g, d).start()
+
+    def filter_sent(g):
+        for d in range(1, SEQ_N):
+            filter_copy(g, d).wait_send()
+
     for g in range(2):
         for d in list(range(1, SEQ_N)) + [0]:
             for part in range(2):
@@ -141,12 +160,10 @@
                             hr[g, me, part, i, pl.ds(cl * 32, 32), :] = val
                         else:
                             hs[g, d, part, i, pl.ds(cl * 32, 32), :] = val
-            if d:
-                copy = pltpu.make_async_remote_copy(
-                    src_ref=hs.at[g, d], dst_ref=hr.at[g, me], send_sem=hs_sem.at[g, d],
-                    recv_sem=hr_sem.at[g, d], device_id=(peer[d], mc), device_id_type=MESH)
-                copy.start()
-                h_out.append(copy)
+        if g == 0:
+            for copy in x_out:
+                copy.wait_send()
+            start_filter(0)
 
     for n in range(3, 8):
         loads[n].wait()
@@ -235,61 +252,89 @@
             copy.wait_recv()
         for cl in range(2):
             c32[cl] = cr[g, :, cl].reshape(512, 128).astype(F32)
-        for cl in range(2):
-            at = (2 * g + cl) * 16
-            gain = gain_col[at:at + 16]
-            for j in range(32):
-                lanes = slice(j * 128, (j + 1) * 128)
-                direct = c32[cl, pl.ds(j, 16, stride=32), :] + gain * sig[at:at + 16, lanes].astype(F32)
-                gt[mc, g, pl.ds(cl * 16, 16), lanes] = (gate[at:at + 16, lanes].astype(F32) * direct).astype(BF)
-
-    gathered = []
+        width = 4096 // CHUNKS[g]
+        for t in range(CHUNKS[g]):
+            for cl in range(2):
+                at = (2 * g + cl) * 16
+                gain = gain_col[at:at + 16]
+                for j in range(t * width // 128, (t + 1) * width // 128):
+                    lanes = slice(j * 128, (j + 1) * 128)
+                    direct = c32[cl, pl.ds(j, 16, stride=32), :] + gain * sig[at:at + 16, lanes].astype(F32)
+                    gt[mz, g, pl.ds(cl * 16, 16), lanes] = (gate[at:at + 16, lanes].astype(F32) * direct).astype(BF)
+            own[g, t] = [pass_on(g, t, mz, every, upc, 0), pass_on(g, t, mz, every, dnc, 1)]
+
+    own, halves, gathered = {}, {}, []
     every, first, second = pl.ds(0, 32), pl.ds(0, 16), pl.ds(16, 16)
-
-    def pass_on(g, block, rows, to, n):
+    zdn, zup = lax.rem(mz + 3, 4), lax.rem(mz + 1, 4)
+
+    def pass_on(g, t, block, rows, to, n):
+        width = 4096 // CHUNKS[g]
+        part = gt.at[block, g, rows, pl.ds(t * width, width)]
         copy = pltpu.make_async_remote_copy(
-            src_ref=gt.at[block, g, rows], dst_ref=gt.at[block, g, rows], send_sem=gs_sem.at[g, n],
-            recv_sem=gr_sem.at[g, n], device_id=(me, to), device_id_type=MESH)
+            src_ref=part, dst_ref=part, send_sem=gs_sem.at[g, t * 4 + n],
+            recv_sem=gr_sem.at[g, t * 4 + n], device_id=(me, to), device_id_type=MESH)
         copy.start()
         gathered.append(copy)
         return copy
 
-    def spread_own(g):
-        return [pass_on(g, mc, every, pc, 0), pass_on(g, mc, every, upc, 1), pass_on(g, mc, every, dnc, 2)]
-
-    def spread_partner(g, own):
-        own[0].wait_recv()
-        partner = [pass_on(g, pc, every, upc, 3), pass_on(g, pc, every, dnc, 4)]
-        own[1].wait_recv()
-        own[2].wait_recv()
-        return partner + [pass_on(g, dnc, first, upc, 5), pass_on(g, upc, second, dnc, 6)]
-
-    def spread_last(g, partner):
-        partner[0].wait_recv()
-        partner[1].wait_recv()
-        return partner[2:] + [pass_on(g, flip(dnc), first, upc, 7), pass_on(g, flip(upc), second, dnc, 8)]
-
+    def send_on(g):
+        for t in range(CHUNKS[g]):
+            own[g, t][0].wait_recv()
+            own[g, t][1].wait_recv()
+            halves[g, t] = [pass_on(g, t, zdn, first, upc, 2), pass_on(g, t, zup, second, dnc, 3)]
+
+    at_k = lax.broadcasted_iota(jnp.int32, (512, 128), 0)
+    at_n = lax.broadcasted_iota(jnp.int32, (512, 128), 1)
+
+    def weights(g):
+        pick = at_k == (at_n // 32) * 128 + xh * 64 + g * 32 + at_n % 32
+        both = jnp.concatenate([w_ref[...], wp[...]], axis=0)
+        return dot(both, jnp.where(pick, 1.0, 0.0).astype(BF)).astype(BF)
+
+    def partial(g, wg, lanes):
+        return dot(wg, gt[:, g, :, lanes].reshape(128, lanes.stop - lanes.start))
+
+    filter_sent(0)
+    start_filter(1)
     inverse_of(0, me)
     lax.fori_loop(1, SEQ_N, inverse_step(0), 0)
     conv_a = inverse_end(0)
     inverse_of(1, me)
-    lax.fori_loop(1, 9, inverse_step(1), 0)
+    lax.fori_loop(1, SPLIT, inverse_step(1), 0)
     gating(0, conv_a)
-    own_a = spread_own(0)
-    lax.fori_loop(9, SEQ_N, inverse_step(1), 0)
+    lax.fori_loop(SPLIT, SEQ_N, inverse_step(1), 0)
     conv_b = inverse_end(1)
-    partner_a = spread_partner(0, own_a)
+    send_on(0)
+    w_copy.wait_recv()
+    w0, w1 = weights(0), weights(1)
     gating(1, conv_b)
-    own_b = spread_own(1)
-    last_a = spread_last(0, partner_a)
-    partner_b = spread_partner(1, own_b)
-    last_b = spread_last(1, partner_b)
-    for copy in last_a + last_b:
+    for copy in halves[0, 0]:
         copy.wait_recv()
     for j in range(8):
         lanes = slice(j * 512, (j + 1) * 512)
-        out_ref[:, lanes] = dot(w_ref[...], gt[:, :, :, lanes].reshape(512, 512)).astype(BF)
-    for copy in x_out + h_out + conv_a + conv_b + gathered:
+        acc[:, lanes] = partial(0, w0, lanes)
+    send_on(1)
+    swaps = []
+    width = 4096 // CHUNKS[1]
+    for t in range(CHUNKS[1]):
+        for copy in halves[1, t]:
+            copy.wait_recv()
+        lanes = slice(t * width, (t + 1) * width)
+        full = acc[:, lanes] + partial(1, w1, lanes)
+        acc[0:64, lanes] = full[:64]
+        ps[:, lanes] = full[64:].astype(BF)
+        part = pl.ds(t * width, width)
+        copy = pltpu.make_async_remote_copy(
+            src_ref=ps.at[:, part], dst_ref=pr.at[:, part], send_sem=ps_sem.at[t], recv_sem=pr_sem.at[t],
+            device_id=(me, pc), device_id_type=MESH)
+        copy.start()
+        swaps.append(copy)
+    for t, copy in enumerate(swaps):
+        copy.wait_recv()
+        lanes = slice(t * width, (t + 1) * width)
+        out_ref[:, lanes] = (acc[0:64, lanes] + pr[:, lanes].astype(F32)).astype(BF)
+    filter_sent(1)
+    for copy in conv_a + conv_b + gathered + swaps + [w_copy]:
         copy.wait_send()
 
 
@@ -311,8 +356,8 @@
             wide(4, 512, 128), buf(16, 4, 32, 128), buf(16, 4, 32, 128),
             buf(2, 16, 2, 2, 64, 128), buf(2, 16, 2, 2, 64, 128), buf(32, 256, 128), wide(32, 256, 128),
             buf(2, 2, 1024, 256), buf(2, 16, 2, 32, 128), buf(2, 16, 2, 32, 128), wide(2, 512, 128),
-            buf(CHAN_N, 2, 32, 4096),
-            dma(14), dma(16), dma(16), dma(2, 16), dma(2, 16), dma(2, 16), dma(2, 16), dma(2, 9), dma(2, 9)],
+            buf(4, 2, 32, 4096), buf(64, 512), wide(128, 4096), buf(64, 4096), buf(64, 4096),
+            dma(14), dma(16), dma(16), dma(2, 16), dma(2, 16), dma(2, 16), dma(2, 16), dma(2, 16), dma(2, 16), dma(5), dma(5)],
         compiler_params=pltpu.CompilerParams(
             collective_id=0, has_side_effects=True, vmem_limit_bytes=60 * 1024 * 1024),
         cost_estimate=pl.CostEstimate(flops=10**10, bytes_accessed=3 * 10**7, transcendentals=0),

time: 86.5 us -> 81.8 us (0.946)
  Pallas kernels: 84.4 us -> 79.7 us
    pallas_call x1, Pallas kernels: 84.4 us -> 79.7 us  [body(): pl.pallas_call(kernel, out_shape=jax.ShapeDtypeStruct((64, 4096), BF), in...]
where the time goes in v3:
time: 81.8 us; the launch traced here: 81.6 us
  Pallas kernels  79.7 us (97%)
  local copies, waits for them, and re-layouts  1.87 us (2%)
    pallas_call x1, Pallas kernels, body(): pl.pallas_call(kernel, out_shape=jax.ShapeDtypeStruct((64, 4096), BF), in...  79.7 us
    unnamed x1, local copies, waits for them, and re-layouts  1.87 us

profile of v3, /device:TPU:0, one launch (start us, length us, event | category | flops | bytes accessed | tf_op | source)
XLA Modules:
  0.0 81.6 jit_solution(2146650022531535681)
XLA Ops:
  0.0 79.7 %shard_map.154 = bf16[64,4096]{1,0:T(8,128)(2,1)} custom-call(bf16[64,4096]{1,0:T(8,128)(2,1)} %sig_hbm.1, bf16[64,4096]{1,0:T(8,128)(2,1)} %gate_hbm.1, f32[4096,128]{1,0:T(8,128)} %bitcast.11, f32[4096,128]{1,0:T(8,128)} %bitcast.12, f32[1,64]{1,0:T(1,128)} %bitcast.13, bf16[64,512]{1,0:T(8,128)(2,1)} %w_ref.1, ...), custom_call_target="tpu_custom_call" | custom-call | flops 10000000000 | bytes 30000000 | tf_op jit(solution)/shard_map/pallas_call | solution.py:350
  79.7 1.9 %copy.20 = bf16[64,4096]{1,0:T(8,128)(2,1)} copy(bf16[64,4096]{1,0:T(8,128)(2,1)} %shard_map.154) | data formatting | bytes 1048576

commit v4 on v3

--- a/solution.py
+++ b/solution.py
@@ -12,7 +12,7 @@
 SEQ_N = 16
 CHAN_N = 8
 CHUNKS = (1, 4)
-SPLIT = 9
+SPLIT = 4
 MESH = pl.DeviceIdType.MESH
 
 
@@ -83,12 +83,12 @@
     return lax.dot_general(a, b, (((1,), (1,)), ((), ())), preferred_element_type=F32)
 
 
-def kernel(sig_hbm, gate_hbm, hre_hbm, him_hbm, gain_ref, w_ref,
+def kernel(sig_hbm, gate_hbm, hre_hbm, him_hbm, gain_ref, w_hbm,
            k0_hbm, k0i_hbm, m_hbm, mi_hbm, tw_hbm, twi_hbm, l2_hbm, l2i_hbm, perm_hbm, permi_hbm,
-           out_ref,
-           sig, gate, h32, k0, k0i, m, mi, tw, twi, l2, l2i, perm, permi,
+           out_hbm,
+           w_ref, out_ref, sig, gate, h32, k0, k0i, m, mi, tw, twi, l2, l2i, perm, permi,
            s32, sx, xr, hs, hr, dsc, fsc, osc, cs, cr, c32, gt, wp, acc, ps, pr,
-           load_sem, xs_sem, xr_sem, hs_sem, hr_sem, cs_sem, cr_sem, gs_sem, gr_sem, ps_sem, pr_sem):
+           load_sem, xs_sem, xr_sem, hs_sem, hr_sem, cs_sem, cr_sem, gs_sem, gr_sem, ps_sem, pr_sem, out_sem):
     me = lax.axis_index("seq")
     mc = lax.axis_index("chan")
     peer = [lax.rem(me + d, SEQ_N) for d in range(SEQ_N)]
@@ -105,7 +105,7 @@
 
     pairs = [(sig_hbm, sig), (hre_hbm, h32.at[0]), (him_hbm, h32.at[1]), (perm_hbm, perm), (k0_hbm, k0),
              (m_hbm, m), (l2_hbm, l2), (tw_hbm, tw), (l2i_hbm, l2i), (twi_hbm, twi), (mi_hbm, mi),
-             (k0i_hbm, k0i), (permi_hbm, permi), (gate_hbm, gate)]
+             (k0i_hbm, k0i), (permi_hbm, permi), (gate_hbm, gate), (w_hbm, w_ref)]
     loads = [pltpu.make_async_copy(a, b, load_sem.at[n]) for n, (a, b) in enumerate(pairs)]
     for copy in loads:
         copy.start()
@@ -128,6 +128,7 @@
         copy.start()
         x_out.append(copy)
     xr[me] = sx[me]
+    loads[14].wait()
     w_copy = pltpu.make_async_remote_copy(
         src_ref=w_ref, dst_ref=wp, send_sem=ps_sem.at[4], recv_sem=pr_sem.at[4],
         device_id=(me, pc), device_id_type=MESH)
@@ -198,21 +199,23 @@
         loads[n].wait()
     low = lax.broadcasted_iota(jnp.int32, (32, 128), 1) < 64
 
-    def inverse_of(g, q):
+    def inverse_of(g, qs):
+        rs = [2 * q + i for q in qs for i in range(2)]
         ps = []
-        for i in range(2):
-            r = 2 * q + i
+        for n, r in enumerate(rs):
             fr = fsc[r, pl.ds(g * 64, 64), :]
             fi = fsc[r, pl.ds(128 + g * 64, 64), :]
-            re, im = hr[g, q, 0, i].astype(F32), hr[g, q, 1, i].astype(F32)
+            re, im = hr[g, qs[n // 2], 0, n % 2].astype(F32), hr[g, qs[n // 2], 1, n % 2].astype(F32)
             ps.append(jnp.concatenate([fr * re - fi * im, fr * im + fi * re], axis=0).astype(BF))
-        gv = dot(l2i[...], jnp.concatenate(ps, axis=1))
-        for i in range(2):
-            r = 2 * q + i
-            gr, gi = gv[:64, i * 128:(i + 1) * 128], gv[64:, i * 128:(i + 1) * 128]
+        gv = [dot(l2i[...], jnp.concatenate(ps[n:n + 2], axis=1)) for n in range(0, len(rs), 2)]
+        os = []
+        for n, r in enumerate(rs):
+            half = gv[n // 2][:, (n % 2) * 128:(n % 2 + 1) * 128]
+            gr, gi = half[:64], half[64:]
             c, s = twi[r, 0], twi[r, 1]
             gc = jnp.concatenate([gr * c - gi * s, gi * c + gr * s], axis=1).astype(BF)
-            o = dot_nt(mi[r], jnp.concatenate([gc, gc], axis=0))
+            os.append(dot_nt(mi[r], jnp.concatenate([gc, gc], axis=0)))
+        for r, o in zip(rs, os):
             for ri in range(2):
                 for k in range(2):
                     at = ri * 128 + k * 64
@@ -222,14 +225,20 @@
                             val[h * 16:(h + 1) * 16])
 
     def inverse_step(g):
-        def step(d, carry):
-            q = lax.rem(me - d + SEQ_N, SEQ_N)
-            pltpu.make_async_remote_copy(
-                src_ref=hs.at[g, d], dst_ref=hr.at[g, q], send_sem=hs_sem.at[g, d],
-                recv_sem=hr_sem.at[g, d], device_id=(me, mc), device_id_type=MESH).wait_recv()
-            inverse_of(g, q)
+        def step(t, carry):
+            for u in range(2):
+                d = 2 * t + u
+                pltpu.make_async_remote_copy(
+                    src_ref=hs.at[g, d], dst_ref=hr.at[g, lax.rem(me - d + SEQ_N, SEQ_N)],
+                    send_sem=hs_sem.at[g, d], recv_sem=hr_sem.at[g, d], device_id=(me, mc),
+                    device_id_type=MESH).wait_recv()
+            inverse_of(g, [lax.rem(me - 2 * t - u + SEQ_N, SEQ_N) for u in range(2)])
             return carry
         return step
+
+    def inverse_first(g):
+        filter_copy(g, 1).wait_recv()
+        inverse_of(g, [me, source[1]])
 
     def inverse_end(g):
         for h in range(2):
@@ -247,6 +256,8 @@
         cr[g, me] = cs[g, me]
         return sent
 
+    own, gathered, done = {}, [], []
+
     def gating(g, arrivals):
         for copy in arrivals:
             copy.wait_recv()
@@ -263,7 +274,7 @@
                     gt[mz, g, pl.ds(cl * 16, 16), lanes] = (gate[at:at + 16, lanes].astype(F32) * direct).astype(BF)
             own[g, t] = [pass_on(g, t, mz, every, upc, 0), pass_on(g, t, mz, every, dnc, 1)]
 
-    own, halves, gathered = {}, {}, []
+    halves = {}
     every, first, second = pl.ds(0, 32), pl.ds(0, 16), pl.ds(16, 16)
     zdn, zup = lax.rem(mz + 3, 4), lax.rem(mz + 1, 4)
 
@@ -277,8 +288,8 @@
         gathered.append(copy)
         return copy
 
-    def send_on(g):
-        for t in range(CHUNKS[g]):
+    def send_on(g, chunks):
+        for t in chunks:
             own[g, t][0].wait_recv()
             own[g, t][1].wait_recv()
             halves[g, t] = [pass_on(g, t, zdn, first, upc, 2), pass_on(g, t, zup, second, dnc, 3)]
@@ -296,15 +307,15 @@
 
     filter_sent(0)
     start_filter(1)
-    inverse_of(0, me)
-    lax.fori_loop(1, SEQ_N, inverse_step(0), 0)
+    inverse_first(0)
+    lax.fori_loop(1, 8, inverse_step(0), 0)
     conv_a = inverse_end(0)
-    inverse_of(1, me)
+    inverse_first(1)
     lax.fori_loop(1, SPLIT, inverse_step(1), 0)
     gating(0, conv_a)
-    lax.fori_loop(SPLIT, SEQ_N, inverse_step(1), 0)
+    lax.fori_loop(SPLIT, 8, inverse_step(1), 0)
     conv_b = inverse_end(1)
-    send_on(0)
+    send_on(0, [0])
     w_copy.wait_recv()
     w0, w1 = weights(0), weights(1)
     gating(1, conv_b)
@@ -313,10 +324,12 @@
     for j in range(8):
         lanes = slice(j * 512, (j + 1) * 512)
         acc[:, lanes] = partial(0, w0, lanes)
-    send_on(1)
     swaps = []
+    send_on(1, [0])
     width = 4096 // CHUNKS[1]
     for t in range(CHUNKS[1]):
+        if t + 1 < CHUNKS[1]:
+            send_on(1, [t + 1])
         for copy in halves[1, t]:
             copy.wait_recv()
         lanes = slice(t * width, (t + 1) * width)
@@ -329,13 +342,20 @@
             device_id=(me, pc), device_id_type=MESH)
         copy.start()
         swaps.append(copy)
+    stores = []
     for t, copy in enumerate(swaps):
         copy.wait_recv()
         lanes = slice(t * width, (t + 1) * width)
         out_ref[:, lanes] = (acc[0:64, lanes] + pr[:, lanes].astype(F32)).astype(BF)
+        copy = pltpu.make_async_copy(out_ref.at[:, lanes], out_hbm.at[:, lanes], out_sem.at[t])
+        copy.start()
+        stores.append(copy)
+    for copy in stores:
+        copy.wait()
     filter_sent(1)
     for copy in conv_a + conv_b + gathered + swaps + [w_copy]:
-        copy.wait_send()
+        if id(copy) not in done:
+            copy.wait_send()
 
 
 def body(signal, gate, spec_real, spec_imag, skip_gain, mix_weight):
@@ -350,14 +370,14 @@
     return pl.pallas_call(
         kernel,
         out_shape=jax.ShapeDtypeStruct((64, 4096), BF),
-        in_specs=[anywhere] * 4 + [vmem] * 2 + [anywhere] * len(consts),
-        out_specs=vmem,
-        scratch_shapes=[buf(64, 4096), buf(64, 4096), wide(2, 4096, 128)] + held + [
+        in_specs=[anywhere] * 4 + [vmem, anywhere] + [anywhere] * len(consts),
+        out_specs=anywhere,
+        scratch_shapes=[buf(64, 512), buf(64, 4096), buf(64, 4096), buf(64, 4096), wide(2, 4096, 128)] + held + [
             wide(4, 512, 128), buf(16, 4, 32, 128), buf(16, 4, 32, 128),
             buf(2, 16, 2, 2, 64, 128), buf(2, 16, 2, 2, 64, 128), buf(32, 256, 128), wide(32, 256, 128),
             buf(2, 2, 1024, 256), buf(2, 16, 2, 32, 128), buf(2, 16, 2, 32, 128), wide(2, 512, 128),
             buf(4, 2, 32, 4096), buf(64, 512), wide(128, 4096), buf(64, 4096), buf(64, 4096),
-            dma(14), dma(16), dma(16), dma(2, 16), dma(2, 16), dma(2, 16), dma(2, 16), dma(2, 16), dma(2, 16), dma(5), dma(5)],
+            dma(15), dma(16), dma(16), dma(2, 16), dma(2, 16), dma(2, 16), dma(2, 16), dma(2, 16), dma(2, 16), dma(5), dma(5), dma(4)],
         compiler_params=pltpu.CompilerParams(
             collective_id=0, has_side_effects=True, vmem_limit_bytes=60 * 1024 * 1024),
         cost_estimate=pl.CostEstimate(flops=10**10, bytes_accessed=3 * 10**7, transcendentals=0),

time: 81.8 us -> 81 us (level)
  no operation moved by 1% of the time
where the time goes in v4:
time: 81 us; the launch traced here: 80.9 us
  Pallas kernels  79 us (98%)
  local copies, waits for them, and re-layouts  1.87 us (2%)
    pallas_call x1, Pallas kernels, body(): pl.pallas_call(kernel, out_shape=jax.ShapeDtypeStruct((64, 4096), BF), in...  79 us
    unnamed x1, local copies, waits for them, and re-layouts  1.87 us

profile of v4, /device:TPU:0, one launch (start us, length us, event | category | flops | bytes accessed | tf_op | source)
XLA Modules:
  0.0 80.9 jit_solution(16871843128067623750)
XLA Ops:
  0.0 79.0 %shard_map.154 = bf16[64,4096]{1,0:T(8,128)(2,1)} custom-call(bf16[64,4096]{1,0:T(8,128)(2,1)} %sig_hbm.1, bf16[64,4096]{1,0:T(8,128)(2,1)} %gate_hbm.1, f32[4096,128]{1,0:T(8,128)} %bitcast.11, f32[4096,128]{1,0:T(8,128)} %bitcast.12, f32[1,64]{1,0:T(1,128)} %bitcast.13, bf16[64,512]{1,0:T(8,128)(2,1)} %w_hbm.1, ...), custom_call_target="tpu_custom_call" | custom-call | flops 10000000000 | bytes 30000000 | tf_op jit(solution)/shard_map/pallas_call | solution.py:370
  79.0 1.9 %copy.20 = bf16[64,4096]{1,0:T(8,128)(2,1)} copy(bf16[64,4096]{1,0:T(8,128)(2,1)} %shard_map.154) | data formatting | bytes 1048576

commit v5 on v4

--- a/solution.py
+++ b/solution.py
@@ -11,7 +11,7 @@
 N = 131072
 SEQ_N = 16
 CHAN_N = 8
-CHUNKS = (1, 4)
+CHUNKS = (2, 4)
 SPLIT = 4
 MESH = pl.DeviceIdType.MESH
 
@@ -315,11 +315,11 @@
     gating(0, conv_a)
     lax.fori_loop(SPLIT, 8, inverse_step(1), 0)
     conv_b = inverse_end(1)
-    send_on(0, [0])
+    send_on(0, [0, 1])
     w_copy.wait_recv()
     w0, w1 = weights(0), weights(1)
     gating(1, conv_b)
-    for copy in halves[0, 0]:
+    for copy in halves[0, 0] + halves[0, 1]:
         copy.wait_recv()
     for j in range(8):
         lanes = slice(j * 512, (j + 1) * 512)

time: 81 us -> 80.5 us (level)
  no operation moved by 1% of the time
where the time goes in v5:
time: 80.5 us; the launch traced here: 80.4 us
  Pallas kernels  78.5 us (98%)
  local copies, waits for them, and re-layouts  1.87 us (2%)
    pallas_call x1, Pallas kernels, body(): pl.pallas_call(kernel, out_shape=jax.ShapeDtypeStruct((64, 4096), BF), in...  78.5 us
    unnamed x1, local copies, waits for them, and re-layouts  1.87 us

profile of v5, /device:TPU:0, one launch (start us, length us, event | category | flops | bytes accessed | tf_op | source)
XLA Modules:
  0.0 80.4 jit_solution(17643872915112157146)
XLA Ops:
  0.0 78.5 %shard_map.154 = bf16[64,4096]{1,0:T(8,128)(2,1)} custom-call(bf16[64,4096]{1,0:T(8,128)(2,1)} %sig_hbm.1, bf16[64,4096]{1,0:T(8,128)(2,1)} %gate_hbm.1, f32[4096,128]{1,0:T(8,128)} %bitcast.11, f32[4096,128]{1,0:T(8,128)} %bitcast.12, f32[1,64]{1,0:T(1,128)} %bitcast.13, bf16[64,512]{1,0:T(8,128)(2,1)} %w_hbm.1, ...), custom_call_target="tpu_custom_call" | custom-call | flops 10000000000 | bytes 30000000 | tf_op jit(solution)/shard_map/pallas_call | solution.py:370
  78.5 1.9 %copy.20 = bf16[64,4096]{1,0:T(8,128)(2,1)} copy(bf16[64,4096]{1,0:T(8,128)(2,1)} %shard_map.154) | data formatting | bytes 1048576
